TPU v7x, 32 devices: a whole 2x2x4 slice. The times are simulated.
32 devices in a mesh: groups: 2 (over y), outer: 2 (over core), inner: 8 (over z, x).
Axes of the slice: x: 2, y: 2, z: 4, core: 2. Of those that a mesh axis runs over, the one named last changes fastest.
Arguments:
- readings: float32 [2048, 16384], P(('groups', 'outer'), 'inner'), parts along dimension 0, may hold values from -6 to 6
- obs_rows: float32 [16384, 16], replicated, may hold values from -0.1875 to 0.1875
- obs_block: int32 [16384], replicated, may hold values from 0 to 15
- sensor_prec: float32 [16384], replicated, may hold values from 0.2 to 5
- prior_mean: float32 [512], P('groups'), parts along dimension 0, may hold values from -5 to 5
- filt_trans: float32 [256, 256], replicated, may hold values from -1 to 1
- model_trans: float32 [256, 256], replicated, may hold values from -1 to 1
- info_gain: float32 [256, 256], replicated, may hold values from -0.01171875 to 0.01171875
- smooth_gain: float32 [256, 256], replicated, may hold values from -1 to 1
Outputs:
- filtered: float32 [2048, 256], P(('groups', 'outer', 'inner')), parts along dimension 0
- smoothed: float32 [2048, 256], P(('groups', 'outer', 'inner')), parts along dimension 0
There are 2 independent parts, one for each index of `groups`. A program takes and returns all parts, laid end to end along the dimension named above; an argument that names none is the same for every part. Nothing has to cross between parts.
All inputs are finite; a program needn't handle non-finite values.
Results may differ from a plain program's by a relative error of at most 0.0003.
Values sent between devices are 32-bit elements; how exact they have to be, the bound alone decides.
A program may use at most 256 MiB of HBM per device.

v0:
```python
import jax
import jax.numpy as jnp
from jax import lax
from jax.sharding import PartitionSpec as P

NS = 256
BLK = 16


highest = lax.Precision.HIGHEST


def entering(part, axis, combine, identity, reverse):
    count = lax.axis_size(axis)
    place = lax.axis_index(axis)
    ahead = count - 1 - place if reverse else place
    gathered = jax.tree.map(lambda a: lax.all_gather(a, axis), part)
    state = jax.tree.map(lambda a, e: jnp.zeros_like(a) + jnp.asarray(e, a.dtype), part, identity)

    def one(turn, state):
        source = count - 1 - turn if reverse else turn
        return combine(
            state, jax.tree.map(lambda a: lax.dynamic_index_in_dim(a, source, 0, False), gathered)
        )

    return lax.fori_loop(0, ahead, one, state)


def matmul(left_side, right_side):
    return jnp.dot(left_side, right_side, precision=highest, preferred_element_type=jnp.float32)


def raise_power(matrix, number):
    result = None
    square = matrix
    remaining = number
    while remaining > 0:
        if remaining % 2 == 1:
            result = square
        remaining = remaining // 2
        if remaining > 0:
            square = matmul(square, square)
    return result


def power_stack(matrix, count):
    power_rows = matrix[None]
    while power_rows.shape[0] < count:
        filled = power_rows.shape[0]
        wanted = min(filled, count - filled)
        highest_power = power_rows[filled - 1]
        extra = jnp.einsum("kij,jl->kil", power_rows, highest_power, precision=highest)
        power_rows = jnp.concatenate([power_rows, extra], axis=0)
    return power_rows


def forward_run(matrix, start_state, drives):

    def advance(carried, drive_row):
        updated = matmul(matrix, carried) + drive_row
        return (updated, updated)

    return lax.scan(advance, start_state, drives)


def backward_run(matrix, start_state, corrections):

    def retreat(carried, correction_row):
        updated = matmul(matrix, carried) + correction_row
        return (updated, updated)

    return lax.scan(retreat, start_state, corrections, reverse=True)


def make_tools(matrix, stretch_len, chain_size):
    stretch_power = raise_power(matrix, stretch_len)
    zero_vector = jnp.zeros((NS,), jnp.float32)
    levels = chain_size.bit_length()
    power_table = [stretch_power]
    for bit_index in range(levels - 1):
        power_table.append(matmul(power_table[-1], power_table[-1]))

    def apply_count(span_count, vector):
        result = vector
        for bit_index in range(levels):
            bit_value = jnp.mod(jnp.floor(span_count / 2.0**bit_index), 2.0)
            result = jnp.where(bit_value > 0.5, matmul(power_table[bit_index], result), result)
        return result

    def combine(earlier, later_part):
        return (earlier[0] + later_part[0], apply_count(later_part[0], earlier[1]) + later_part[1])

    def element(vector):
        return (jnp.ones((), jnp.float32), vector)

    identity = (jnp.zeros((), jnp.float32), zero_vector)

    def apply_to(prefix, start_state):
        return apply_count(prefix[0], start_state) + prefix[1]

    return (element, combine, identity, apply_to)


def chain_prefix(own_element, combine, identity, backward):
    return entering(own_element, ("outer", "inner"), combine, identity, backward)


def on_device(
    readings,
    obs_rows,
    obs_block,
    sensor_prec,
    prior_mean,
    filt_trans,
    model_trans,
    info_gain,
    smooth_gain,
):
    blocks = NS // BLK
    one_hot = (obs_block[:, None] == jnp.arange(blocks, dtype=jnp.int32)[None, :]).astype(
        jnp.float32
    )
    obs_full = (one_hot[:, :, None] * obs_rows[:, None, :]).reshape(obs_rows.shape[0], NS)
    regrouped = lax.all_to_all(readings, "inner", split_axis=0, concat_axis=1, tiled=True)
    weighted = regrouped * sensor_prec[None, :]
    information = matmul(weighted, obs_full)
    drives = matmul(information, info_gain.T)
    steps_here = drives.shape[0]
    chain_size = lax.axis_size("outer") * lax.axis_size("inner")
    zero_vector = jnp.zeros((NS,), jnp.float32)
    filter_element, filter_combine, filter_identity, filter_apply = make_tools(
        filt_trans, steps_here, chain_size
    )
    local_end, local_states = forward_run(filt_trans, zero_vector, drives)
    prefix_in = chain_prefix(filter_element(local_end), filter_combine, filter_identity, False)
    entry_state = filter_apply(prefix_in, prior_mean)
    filter_powers = power_stack(filt_trans, steps_here)
    filtered = local_states + jnp.einsum("kij,j->ki", filter_powers, entry_state, precision=highest)
    predicted = matmul(matmul(filtered, model_trans.T), smooth_gain.T)
    is_final = jnp.logical_and(
        lax.axis_index("outer") == lax.axis_size("outer") - 1,
        lax.axis_index("inner") == lax.axis_size("inner") - 1,
    )
    last_row = (jnp.arange(steps_here, dtype=jnp.int32) == steps_here - 1)[:, None]
    corrections = jnp.where(jnp.logical_and(is_final, last_row), filtered, filtered - predicted)
    smooth_element, smooth_combine, smooth_identity, smooth_apply = make_tools(
        smooth_gain, steps_here, chain_size
    )
    local_head, local_back = backward_run(smooth_gain, zero_vector, corrections)
    prefix_out = chain_prefix(smooth_element(local_head), smooth_combine, smooth_identity, True)
    exit_state = smooth_apply(prefix_out, zero_vector)
    smooth_powers = power_stack(smooth_gain, steps_here)[::-1]
    smoothed = local_back + jnp.einsum("kij,j->ki", smooth_powers, exit_state, precision=highest)
    return (filtered, smoothed)


def solution(mesh):
    placed = (P(("groups", "outer"), "inner"), P(), P(), P(), P("groups"), P(), P(), P(), P())
    return jax.shard_map(
        on_device,
        mesh=mesh,
        in_specs=placed,
        out_specs=(P(("groups", "outer", "inner"), None), P(("groups", "outer", "inner"), None)),
        check_vma=False,
    )
```

profile of v0, /device:TPU:0, one launch (start us, length us, event | category | flops | bytes accessed | tf_op | source)
XLA Modules:
  0.0 589.8 jit_solution(2608113557807159623)
XLA Ops:
  0.7 7.4 %all-to-all-start = ((f32[8,64,2048]{2,1,0:T(8,128)}), f32[8,64,2048]{2,1,0:T(8,128)}, u32[]{:S(2)}, u32[]{:S(2)}) async-start(f32[8,64,2048]{2,1,0:T(8,128)} %bitcast.367), calls=%async_computation | async-start | bytes 8388608 | tf_op jit(solution)/shard_map/all_to_all | solution.py:124
  8.1 0.9 constant_dynamic-update-slice_fusion.27
  9.0 1.3 constant_dynamic-update-slice_fusion.26
  12.9 1.0 constant_dynamic-update-slice_fusion.10
  13.9 1.3 constant_dynamic-update-slice_fusion.9
  19.3 0.8 dynamic-update-slice
  20.1 104.3 %all-reduce = f32[16]{0:T(128)} all-reduce(f32[16]{0:T(128)S(1)} %dynamic-update-slice), channel_id=1, replica_groups=mesh['groups'=2,'outer'=2,'inner'=8] {'outer','inner'}, use_global_device_ids=true, to_apply=%add | all-reduce | flops 16 | bytes 128
  124.4 0.9 fusion.74
  126.9 2.8 constant_dynamic-update-slice_fusion.25
  129.7 3.6 constant_dynamic-update-slice_fusion.24
  133.3 4.4 constant_dynamic-update-slice_fusion.23
  137.7 8.9 %constant_dynamic-update-slice_fusion.22 = (f32[32,256,256]{2,1,0:T(8,128)}, f32[64,256,256]{2,1,0:T(8,128)}, f32[16,256,256]{2,1,0:T(8,128)S(1)}) fusion(f32[32,256,256]{2,1,0:T(8,128)} %get-tuple-element.446, f32[64,256,256]{2,1,0:T(8,128)} %get-tuple-element.447, f32[16,256,256]{2,1,0:T(8,128)} %get-tuple-element.448, ...), kind=kOutput, calls=%fused_computation.94 | convolution fusion | flops 3221225472 | bytes 17039360 | tf_op jit(solution)/shard_map/kij,jl->kil/dot_general | solution.py:52
  146.6 11.0 %convolution_dynamic-update-slice_fusion = f32[64,256,256]{2,1,0:T(8,128)} fusion(f32[64,256,256]{2,1,0:T(8,128)} %get-tuple-element.443, f32[32,256,256]{2,1,0:T(8,128)} %get-tuple-element.442, f32[16,256,256]{2,1,0:T(8,128)S(1)} %get-tuple-element.485), kind=kOutput, calls=%fused_computation.17 | convolution fusion | flops 6442450944 | bytes 17039360 | tf_op jit(solution)/shard_map/kij,jl->kil/dot_general | solution.py:52
  157.6 11.8 %rev.3 = f32[64,256,256]{2,1,0:T(8,128)} reverse(f32[64,256,256]{2,1,0:T(8,128)} %convolution_dynamic-update-slice_fusion), dimensions={0} | reverse | bytes 33554432 | tf_op jit(solution)/shard_map/rev | solution.py:152
  169.4 2.7 constant_dynamic-update-slice_fusion.8
  172.2 3.6 constant_dynamic-update-slice_fusion.7
  175.8 5.4 constant_dynamic-update-slice_fusion.6
  181.2 8.9 %constant_dynamic-update-slice_fusion.5 = (f32[32,256,256]{2,1,0:T(8,128)}, f32[64,256,256]{2,1,0:T(8,128)}, f32[16,256,256]{2,1,0:T(8,128)S(1)}) fusion(f32[32,256,256]{2,1,0:T(8,128)} %get-tuple-element.449, f32[64,256,256]{2,1,0:T(8,128)} %get-tuple-element.450, f32[16,256,256]{2,1,0:T(8,128)} %get-tuple-element.451, ...), kind=kOutput, calls=%fused_computation.77 | convolution fusion | flops 3221225472 | bytes 17039360 | tf_op jit(solution)/shard_map/kij,jl->kil/dot_general | solution.py:52
  190.1 11.2 %convolution_dynamic-update-slice_fusion.1 = f32[64,256,256]{2,1,0:T(8,128)} fusion(f32[64,256,256]{2,1,0:T(8,128)} %get-tuple-element.445, f32[32,256,256]{2,1,0:T(8,128)} %get-tuple-element.444, f32[16,256,256]{2,1,0:T(8,128)S(1)} %get-tuple-element.480), kind=kOutput, calls=%fused_computation.18 | convolution fusion | flops 6442450944 | bytes 17039360 | tf_op jit(solution)/shard_map/kij,jl->kil/dot_general | solution.py:52
  201.4 7.6 %broadcast_multiply_fusion = f32[16384,16,16]{0,2,1:T(8,128)} fusion(f32[16384,16]{0,1:T(8,128)S(1)} %copy-done.7, f32[16384,16]{0,1:T(8,128)S(1)} %fusion.29), kind=kLoop, calls=%fused_computation.16 | loop fusion | flops 4194304 | bytes 18874368 | tf_op jit(solution)/shard_map/mul | solution.py:123
  209.1 2.7 multiply_bitcast_fusion
  212.2 3.8 copy-done.1
  216.1 15.6 %fusion.63 = f32[64,256]{1,0:T(8,128)S(1)} fusion(f32[64,16384]{1,0:T(8,128)S(1)} %bitcast.360, f32[16384,256]{0,1:T(8,128)S(1)} %bitcast.353), kind=kOutput, calls=%fused_computation.142 | convolution fusion | flops 3221225472 | bytes 21037056 | tf_op jit(solution)/shard_map/dot_general | solution.py:30
  232.1 27.4 %while.58 = (s32[]{:T(128)}, f32[256]{0:T(256)S(1)}, f32[64,256]{1,0:T(8,128)S(1)}, f32[256,256]{1,0:T(8,128)S(1)}, f32[64,256]{1,0:T(8,128)S(1)}, /*index=5*/s32[]{:T(128)}, s32[]{:T(128)}) while((s32[]{:T(128)}, f32[256]{0:T(256)S(1)}, f32[64,256]{1,0:T(8,128)S(1)}, f32[256,256]{1,0:T(8,128)S(1)}, f32[64,256]{1,0:T(8,128)S(1)}, ...), condition=%wide.region_1.2_spmd.clone, body=%wide.region_0.1_spmd.clone.sunk | while | flops 786947 | bytes 273503 | solution.py:63
  259.4 28.7 %all-gather.2 = f32[16,1,256]{2,1,0:T(1,128)S(1)} all-gather(f32[1,1,256]{2,1,0:T(1,128)S(1)} %bitcast.381), channel_id=2, replica_groups=mesh['groups'=2,'outer'=2,'inner'=8] {'outer','inner'}, dimensions={0}, use_global_device_ids=true | all-gather | bytes 17408 | tf_op jit(solution)/shard_map/all_gather | solution.py:17
  289.8 17.6 %fusion.79 = f32[1,64,256]{2,0,1:T(1,128)S(1)} fusion(f32[64,256,256]{2,1,0:T(8,128)} %convolution_dynamic-update-slice_fusion.1, f32[256,1,1]{0,1,2:T(1,128)S(1)} %bitcast.420), kind=kOutput, calls=%fused_computation.158 | convolution fusion | flops 50331648 | bytes 16843776 | tf_op jit(solution)/shard_map/kij,j->ki/dot_general | solution.py:138
  308.3 26.5 %while.59 = (s32[]{:T(128)}, f32[256]{0:T(256)S(1)}, f32[64,256]{1,0:T(8,128)S(1)}, f32[256,256]{1,0:T(8,128)S(1)}, f32[64,256]{1,0:T(8,128)S(1)}, /*index=5*/s32[]{:T(128)}, s32[]{:T(128)}, s32[]{:T(128)}) while((s32[]{:T(128)}, f32[256]{0:T(256)S(1)}, f32[64,256]{1,0:T(8,128)S(1)}, f32[256,256]{1,0:T(8,128)S(1)}, ...), condition=%wide.region_5.6_spmd.clone, body=%wide.region_4.5_spmd.clone.sunk | while | flops 786948 | bytes 273523 | solution.py:72
  334.8 137.0 %all-gather.3 = f32[16,1,256]{2,1,0:T(1,128)S(1)} all-gather(f32[1,1,256]{2,1,0:T(1,128)S(1)} %bitcast.379), channel_id=3, replica_groups=mesh['groups'=2,'outer'=2,'inner'=8] {'outer','inner'}, dimensions={0}, use_global_device_ids=true | all-gather | bytes 17408 | tf_op jit(solution)/shard_map/all_gather | solution.py:17
  471.8 97.4 %while.57 = (s32[]{:T(128)}, f32[]{:T(128)}, f32[256]{0:T(256)S(1)}, s32[]{:T(128)}, f32[16]{0:T(128)S(1)}, /*index=5*/f32[256,256]{1,0:T(8,128)S(1)}, f32[256,2...) while((s32[]{:T(128)}, f32[]{:T(128)}, ...), condition=%wide.region_7.8_spmd, body=%wide.region_6.7_spmd.sunk | while | flops 3933747 | bytes 1340083 | solution.py:26
  471.8 0.6 dynamic_slice.50
  570.8 17.9 %fusion.94 = f32[1,64,256]{2,0,1:T(1,128)S(1)} fusion(f32[64,256,256]{2,1,0:T(8,128)} %rev.3, f32[256,1,1]{0,1,2:T(1,128)S(1)} %bitcast.423), kind=kOutput, calls=%fused_computation.173 | convolution fusion | flops 50331648 | bytes 16843776 | tf_op jit(solution)/shard_map/kij,j->ki/dot_general | solution.py:153
  588.7 0.6 bitcast_add_fusion
  (907 shorter events, 90.5 us)
Async XLA Ops:
  0.6 231.1 %copy-start = (f32[256,256]{1,0:T(8,128)S(1)}, f32[256,256]{1,0:T(8,128)}, u32[]{:S(2)}) copy-start(f32[256,256]{1,0:T(8,128)} %param.24) | copy-start | bytes 786436
  0.6 7.4 %copy-start.2 = (f32[256,256]{1,0:T(8,128)S(1)}, f32[256,256]{1,0:T(8,128)}, u32[]{:S(2)}) copy-start(f32[256,256]{1,0:T(8,128)} %param.25) | copy-start | bytes 786436
  0.7 12.2 %copy-start.3 = (f32[256,256]{1,0:T(8,128)S(1)}, f32[256,256]{1,0:T(8,128)}, u32[]{:S(2)}) copy-start(f32[256,256]{1,0:T(8,128)} %param.22) | copy-start | bytes 786436
  0.7 208.4 %all-to-all-start = ((f32[8,64,2048]{2,1,0:T(8,128)}), f32[8,64,2048]{2,1,0:T(8,128)}, u32[]{:S(2)}, u32[]{:S(2)}) async-start(f32[8,64,2048]{2,1,0:T(8,128)} %bitcast.367), calls=%async_computation | async-start | bytes 8388608 | tf_op jit(solution)/shard_map/all_to_all | solution.py:124
  9.0 9.7 %copy-start.15 = (u32[32]{0:T(128)S(1)}, u32[32]{0:T(128)}, u32[]{:S(2)}) copy-start(u32[32]{0:T(128)} %constant.208) | copy-start | bytes 388
  9.0 115.3 %copy-start.11 = (f32[16384]{0:T(1024)S(1)}, f32[16384]{0:T(1024)}, u32[]{:S(2)}) copy-start(f32[16384]{0:T(1024)} %param.20) | copy-start | bytes 196612
  9.0 115.3 %copy-start.12 = (f32[256]{0:T(256)S(1)}, f32[256]{0:T(256)}, u32[]{:S(2)}) copy-start(f32[256]{0:T(256)} %param.21) | copy-start | bytes 3076
  10.3 7.6 %copy-start.5 = (f32[256,256]{1,0:T(8,128)}, f32[256,256]{1,0:T(8,128)S(1)}, u32[]{:S(2)}) copy-start(f32[256,256]{1,0:T(8,128)S(1)} %get-tuple-element.481) | copy-start | bytes 786436
  15.2 111.0 %copy-start.4 = (f32[256,256]{1,0:T(8,128)}, f32[256,256]{1,0:T(8,128)S(1)}, u32[]{:S(2)}) copy-start(f32[256,256]{1,0:T(8,128)S(1)} %get-tuple-element.476) | copy-start | bytes 786436
  125.2 8.1 %copy-start.6 = (f32[256,256]{1,0:T(8,128)S(1)}, f32[256,256]{1,0:T(8,128)}, u32[]{:S(2)}) copy-start(f32[256,256]{1,0:T(8,128)} %copy-done.5) | copy-start | bytes 786436
  190.1 11.3 %copy-start.10 = (s32[16384]{0:T(1024)S(1)}, s32[16384]{0:T(1024)}, u32[]{:S(2)}) copy-start(s32[16384]{0:T(1024)} %param.19) | copy-start | bytes 196612
  190.1 11.3 %copy-start.7 = (f32[16384,16]{0,1:T(8,128)S(1)}, f32[16384,16]{0,1:T(8,128)}, u32[]{:S(2)}) copy-start(f32[16384,16]{0,1:T(8,128)} %param.18) | copy-start | bytes 3145732
  209.1 7.0 %copy-start.1 = (f32[16384,16,16]{0,2,1:T(8,128)S(1)}, f32[16384,16,16]{0,2,1:T(8,128)}, u32[]{:S(2)}) copy-start(f32[16384,16,16]{0,2,1:T(8,128)} %broadcast_multiply_fusion) | copy-start | bytes 50331652
  289.8 17.7 %copy-start.9 = (f32[256,256]{1,0:T(8,128)S(1)}, f32[256,256]{1,0:T(8,128)}, u32[]{:S(2)}) copy-start(f32[256,256]{1,0:T(8,128)} %param.23) | copy-start | bytes 786436
  289.8 18.1 %copy-start.13 = (pred[64]{0:T(512)(128)(4,1)S(1)}, pred[64]{0:T(512)(128)(4,1)}, u32[]{:S(2)}) copy-start(pred[64]{0:T(512)(128)(4,1)} %compare_and_fusion) | copy-start | bytes 196
  289.8 182.0 %copy-start.14 = (f32[16]{0:T(128)S(1)}, f32[16]{0:T(128)}, u32[]{:S(2)}) copy-start(f32[16]{0:T(128)} %get-tuple-element.862) | copy-start | bytes 196
  307.5 281.2 %copy-start.8 = (f32[64,256]{1,0:T(8,128)}, f32[64,256]{1,0:T(8,128)S(1)}, u32[]{:S(2)}) copy-start(f32[64,256]{1,0:T(8,128)S(1)} %bitcast_add_fusion.1) | copy-start | bytes 196612
where the time goes:
time: 596 us; the launch traced here: 590 us
  blocking collectives  270 us (45%)
  matrix products  183 us (31%)
  loops' own time  72.8 us (12%)
  local copies, waits for them, and re-layouts  40.9 us (7%)
  other arithmetic  13.5 us (2%)
  starting transfers between devices  7.4 us (1%)
    all_gather x2, blocking collectives, entering(): gathered = jax.tree.map(lambda a: lax.all_gather(a, axis), part)  166 us
    unnamed x1, blocking collectives  104 us
    dot_general x235, matrix products, matmul(): jnp.dot(left_side, right_side, precision=highest, preferred_element_type=...  82.4 us
    another operation x2, loops' own time, entering(): return lax.fori_loop(0, ahead, one, state)  67.3 us
    dot_general x12, matrix products, power_stack(): jnp.einsum('kij,jl->kil', power_rows, highest_power, precision=highest)  65.1 us
    dot_general x1, matrix products, on_device(): jnp.einsum('kij,j->ki', smooth_powers, exit_state, precision=highest)  17.9 us
    dot_general x1, matrix products, on_device(): jnp.einsum('kij,j->ki', filter_powers, entry_state, precision=highest)  17.6 us
  transfers between devices with their start and end apart: 1, of which 0 were waited for; matrix products, arithmetic and copies ran while one was open for 16% of the time, Pallas kernels for 0%

commit v1 on v0

v1 whole, which is shorter than its diff:
```python
import functools

import jax
import jax.numpy as jnp
from jax import lax
from jax.experimental import pallas as pl
from jax.experimental.pallas import tpu as pltpu
from jax.sharding import PartitionSpec as P

MESH = pl.DeviceIdType.MESH
F32 = jnp.float32
BF16 = jnp.bfloat16
KU, KQ, KD, KP, KW = range(5)
MGAIN, MCORR, MEXIT, MMODEL, MWIN = range(5)


def split(x):
    high = x.astype(BF16)
    low = (x - high.astype(F32)).astype(BF16)
    return high, low


def dot(a, b):
    return jnp.dot(a, b, preferred_element_type=F32)


def dot3(a, b):
    return dot(a[0], b[0]) + (dot(a[1], b[0]) + dot(a[0], b[1]))


def exact(a, b):
    return jnp.dot(a, b, precision=lax.Precision.HIGHEST, preferred_element_type=F32)


def first_rows(x, m):
    return jnp.where(lax.broadcasted_iota(jnp.int32, x.shape, 0) < m, x, 0.0)


def halves(x, m):
    if m >= 16:
        return x[:m], x[m:]
    return first_rows(x, m), first_rows(pltpu.roll(x, 16 - m, 0), m)


def stack(top, below, m):
    if m >= 16:
        return jnp.concatenate([top, below], axis=0)
    return top + pltpu.roll(below, m, 0)


def shift_down(x, k):
    return jnp.concatenate([jnp.zeros((k, x.shape[1]), F32), x[:-k]], axis=0)


def shift_up(x, k):
    return jnp.concatenate([x[k:], jnp.zeros((k, x.shape[1]), F32)], axis=0)


def bit_reversed(t, bits):
    return int(format(t, "0%db" % bits)[::-1], 2) if bits else 0


def kernel(
    n_out, n_in, readings, obs_t, block, prec, prior, filt, model, gain, smooth,
    filtered, smoothed,
    chunk, obs_v, obs_w, part, landed, info, lev, dev, misc, pf, qf, wf, mine, ends, pick, kept, leaf,
    in_sem, obs_sem, send_sem, recv_sem, esend_sem, erecv_sem,
):
    n = n_out * n_in
    steps, ns = filtered.shape
    sensors = obs_v.shape[1]
    blk = obs_v.shape[0]
    levels = steps.bit_length() - 1
    dev_levels = n.bit_length() - 1
    inner = lax.axis_index("inner")
    place = lax.axis_index("outer") * n_in + inner

    def target(k):
        q = lax.rem(place + k, n)
        return {"outer": q // n_in, "inner": lax.rem(q, n_in)}

    barrier = pltpu.get_barrier_semaphore()

    def greet(k, c):
        pl.semaphore_signal(barrier, inc=1, device_id=target(k), device_id_type=MESH)
        return c

    lax.fori_loop(1, n, greet, 0)

    obs_copy = pltpu.make_async_copy(
        obs_t.at[:, pl.ds(pl.multiple_of(inner * sensors, sensors), sensors)], obs_v, obs_sem
    )
    obs_copy.start()

    def in_copy(k):
        dest = lax.rem(inner + k + 1, n_in)
        return pltpu.make_async_copy(
            readings.at[pl.ds(pl.multiple_of(dest * steps, steps), steps), :],
            chunk.at[k],
            in_sem.at[k],
        )

    def start_in(k, c):
        in_copy(k).start()
        return c

    lax.fori_loop(0, n_in, start_in, 0)
    obs_copy.wait()

    per_row = sensors // 128

    def lane_row(ref):
        return jnp.concatenate(
            [ref[pl.ds(inner * per_row + r, 1), :] for r in range(per_row)], axis=1
        )

    scaled = obs_v[...] * lane_row(prec)
    which = lane_row(block)
    for b in range(ns // blk):
        high, low = split(jnp.where(which == b, scaled, 0.0))
        obs_w[0, b * blk : (b + 1) * blk, :] = high
        obs_w[1, b * blk : (b + 1) * blk, :] = low

    def nt(a, b):
        return lax.dot_general(a, b, (((1,), (1,)), ((), ())), preferred_element_type=F32)

    def rs_copy(k):
        return pltpu.make_async_remote_copy(
            src_ref=part.at[k],
            dst_ref=landed.at[k],
            send_sem=send_sem.at[k],
            recv_sem=recv_sem.at[k],
            device_id={"inner": lax.rem(inner + k + 1, n_in)},
            device_id_type=MESH,
        )

    def partial_sum(k):
        in_copy(k).wait()
        high, low = split(chunk[k])
        part[k] = nt(high, obs_w[0]) + (nt(low, obs_w[0]) + nt(high, obs_w[1]))

    pl.semaphore_wait(barrier, n - 1)

    def reduce_step(k, c):
        partial_sum(k)
        rs_copy(k).start()
        return c

    lax.fori_loop(0, n_in - 1, reduce_step, 0)
    partial_sum(n_in - 1)

    def put(ref, where, value):
        high, low = split(value)
        ref[where + (0,)] = high
        ref[where + (1,)] = low

    trans = filt[...].T
    back = smooth[...].T
    model_t = model[...].T
    put(misc, (MGAIN,), gain[...].T)
    put(misc, (MMODEL,), model_t)
    corr = -exact(model_t, back)
    eye = (
        lax.broadcasted_iota(jnp.int32, (ns, ns), 0) == lax.broadcasted_iota(jnp.int32, (ns, ns), 1)
    )
    corr = jnp.where(eye, corr + 1.0, corr)
    put(misc, (MCORR,), corr)
    pf[...] = trans
    qf[...] = back
    wf[...] = exact(trans, corr)
    start = exact(jnp.broadcast_to(prior[...], (16, ns)), trans)[0:1]

    def grow(k, c):
        p, q, w = pf[...], qf[...], wf[...]
        p2, q2, w2 = split(p), split(q), split(w)
        d2 = split(dot3(p2, w2))
        for kind, pair in ((KU, split(dot3(w2, q2))), (KQ, q2), (KD, d2), (KP, p2), (KW, w2)):
            lev[k, 0, kind * ns : (kind + 1) * ns, :] = pair[0]
            lev[k, 1, kind * ns : (kind + 1) * ns, :] = pair[1]
        wf[...] = w + dot3(d2, q2)
        pf[...] = exact(p, p)
        qf[...] = exact(q, q)
        return c

    lax.fori_loop(0, levels, grow, 0)
    put(misc, (MWIN,), wf[...])
    put(misc, (MEXIT,), exact(model_t, qf[...]))

    def grow_dev(k, c):
        p, q = pf[...], qf[...]
        put(dev, (k, 0), p)
        put(dev, (k, 1), q)
        pf[...] = exact(p, p)
        qf[...] = exact(q, q)
        return c

    lax.fori_loop(0, dev_levels, grow_dev, 0)

    def mul(x2, ref, *where):
        return dot3(x2, (ref[where + (0,)], ref[where + (1,)]))

    def step(x2, k, kind):
        here = slice(kind * ns, kind * ns + x2[0].shape[1])
        return dot3(x2, (lev[k, 0, here, :], lev[k, 1, here, :]))

    def beside(a, b):
        return tuple(jnp.concatenate([u, v], axis=1) for u, v in zip(a, b))

    info[...] = part[n_in - 1]

    def take(k, c):
        rs_copy(k).wait_recv()
        info[...] += landed[k]
        return c

    lax.fori_loop(0, n_in - 1, take, 0)
    drive = mul(split(info[...]), misc, MGAIN)
    first = jnp.where(place == 0, 1.0, 0.0)
    top = lax.broadcasted_iota(jnp.int32, (steps, 1), 0) == 0
    drive = drive + jnp.where(jnp.logical_and(top, first > 0.5), start, 0.0)
    info[...] = drive
    for t in range(steps):
        r = bit_reversed(t, levels)
        leaf[0, r : r + 1, :] = info[t : t + 1, :]
    leaf[1] = mul(split(leaf[0]), misc, MCORR)
    drive, head = leaf[0], leaf[1]

    e, h = drive, head
    spot = [0]
    for k in range(levels):
        m = steps >> (k + 1)
        (el, er), (hl, hr) = halves(e, m), halves(h, m)
        el2, hr2 = split(el), split(hr)
        e = er + step(el2, k, KP)
        h = hl + step(beside(el2, hr2), k, KU)
        here = pl.ds(spot[-1], el.shape[0])
        kept[0, here, :] = el
        kept[1, here, :] = hr + step(el2, k, KW)
        spot.append(spot[-1] + el.shape[0])

    half = ns // 2
    for ref in (mine, ends.at[place]):
        ref[0:1, :] = e[0:1, :half]
        ref[1:2, :] = e[0:1, half:]
        ref[2:3, :] = h[0:1, :half]
        ref[3:4, :] = h[0:1, half:]

    def end_copy(k):
        return pltpu.make_async_remote_copy(
            src_ref=mine,
            dst_ref=ends.at[place],
            send_sem=esend_sem.at[k],
            recv_sem=erecv_sem.at[k],
            device_id=target(k),
            device_id_type=MESH,
        )

    def end_arrival(k):
        q = lax.rem(place - k + n, n)
        return pltpu.make_async_remote_copy(
            src_ref=mine,
            dst_ref=ends.at[q],
            send_sem=esend_sem.at[k],
            recv_sem=erecv_sem.at[k],
            device_id=target(k),
            device_id_type=MESH,
        )

    def send_end(k, c):
        end_copy(k).start()
        return c

    lax.fori_loop(1, n, send_end, 0)

    def take_end(k, c):
        end_arrival(k).wait_recv()
        return c

    lax.fori_loop(1, n, take_end, 0)

    x = jnp.concatenate([ends[:, 0, :], ends[:, 1, :]], axis=1)
    s = jnp.concatenate([ends[:, 2, :], ends[:, 3, :]], axis=1)
    for k in range(dev_levels):
        x = x + shift_down(mul(split(x), dev, k, 0), 1 << k)
    x2 = split(x)
    last = lax.broadcasted_iota(jnp.int32, (n, 1), 0) == n - 1
    s = s + shift_down(mul(x2, misc, MWIN), 1) + jnp.where(last, mul(x2, misc, MEXIT), 0.0)
    for k in range(dev_levels):
        s = s + shift_up(mul(split(s), dev, k, 1), 1 << k)
    pick[0] = shift_down(x, 1)
    pick[1] = jnp.where(last, mul(x2, misc, MMODEL), shift_up(s, 1))
    x = first_rows(jnp.broadcast_to(pick[0, pl.ds(place, 1), :], (16, ns)), 1)
    s = first_rows(jnp.broadcast_to(pick[1, pl.ds(place, 1), :], (16, ns)), 1)

    for k in range(levels - 1, -1, -1):
        m = steps >> (k + 1)
        here = pl.ds(spot[k], spot[k + 1] - spot[k])
        el, g = kept[0, here, :], kept[1, here, :]
        x2, s2 = split(x), split(s)
        xr = el + step(x2, k, KP)
        sl = g + step(beside(s2, x2), k, KQ)
        x = stack(x, xr, m)
        s = stack(sl, s, m)
    x2 = split(x)
    f_rows = leaf[0] + step(x2, 0, KP)
    s_rows = leaf[1] + (step(x2, 0, KW) + step(split(s), 0, KQ))
    for t in range(steps):
        r = bit_reversed(t, levels)
        filtered[t : t + 1, :] = f_rows[r : r + 1, :]
        smoothed[t : t + 1, :] = s_rows[r : r + 1, :]

    def drain(k, c):
        rs_copy(k).wait_send()
        return c

    lax.fori_loop(0, n_in - 1, drain, 0)

    def drain_end(k, c):
        end_copy(k).wait_send()
        return c

    lax.fori_loop(1, n, drain_end, 0)


def on_device(
    readings, obs_rows, obs_block, sensor_prec, prior_mean, filt_trans, model_trans, info_gain, smooth_gain
):
    n_out, n_in = lax.axis_size("outer"), lax.axis_size("inner")
    n = n_out * n_in
    rows, sensors = readings.shape
    steps = rows // n_in
    ns = filt_trans.shape[0]
    blk = obs_rows.shape[1]
    total = obs_rows.shape[0]
    levels = steps.bit_length() - 1
    dev_levels = n.bit_length() - 1
    vmem = pl.BlockSpec(memory_space=pltpu.VMEM)
    hbm = pl.BlockSpec(memory_space=pl.ANY)
    dma = pltpu.SemaphoreType.DMA
    return pl.pallas_call(
        functools.partial(kernel, n_out, n_in),
        out_shape=[jax.ShapeDtypeStruct((steps, ns), F32)] * 2,
        in_specs=[hbm, hbm] + [vmem] * 7,
        out_specs=[vmem, vmem],
        scratch_shapes=[
            pltpu.VMEM((n_in, steps, sensors), F32),
            pltpu.VMEM((blk, sensors), F32),
            pltpu.VMEM((2, ns, sensors), BF16),
            pltpu.VMEM((n_in, steps, ns), F32),
            pltpu.VMEM((n_in - 1, steps, ns), F32),
            pltpu.VMEM((steps, ns), F32),
            pltpu.VMEM((levels, 2, 5 * ns, ns), BF16),
            pltpu.VMEM((dev_levels, 2, 2, ns, ns), BF16),
            pltpu.VMEM((5, 2, ns, ns), BF16),
            pltpu.VMEM((ns, ns), F32),
            pltpu.VMEM((ns, ns), F32),
            pltpu.VMEM((ns, ns), F32),
            pltpu.VMEM((8, ns // 2), F32),
            pltpu.VMEM((n, 8, ns // 2), F32),
            pltpu.VMEM((2, n, ns), F32),
            pltpu.VMEM((2, steps + 16 * levels, ns), F32),
            pltpu.VMEM((2, steps, ns), F32),
            dma((n_in,)),
            dma(()),
            dma((n_in - 1,)),
            dma((n_in - 1,)),
            dma((n,)),
            dma((n,)),
        ],
        compiler_params=pltpu.CompilerParams(
            collective_id=0, has_side_effects=True, vmem_limit_bytes=56 * 1024 * 1024
        ),
        name="smoother",
    )(
        readings,
        obs_rows.T,
        obs_block.reshape(total // 128, 128),
        sensor_prec.reshape(total // 128, 128),
        prior_mean.reshape(1, ns),
        filt_trans,
        model_trans,
        info_gain,
        smooth_gain,
    )


def solution(mesh):
    placed = (P(("groups", "outer"), "inner"), P(), P(), P(), P("groups"), P(), P(), P(), P())
    return jax.shard_map(
        on_device,
        mesh=mesh,
        in_specs=placed,
        out_specs=(P(("groups", "outer", "inner"), None), P(("groups", "outer", "inner"), None)),
        check_vma=False,
    )
```

time: 596 us -> 39.2 us (0.07); the launches traced: 590 us -> 39 us
  blocking collectives: 270 us -> 0 us
  matrix products: 183 us -> 0 us
  loops' own time: 72.8 us -> 0 us
  local copies, waits for them, and re-layouts: 40.9 us -> 2.95 us
  Pallas kernels: 0 us -> 35.4 us
  other arithmetic: 13.5 us -> 0 us
  starting transfers between devices: 7.4 us -> 0 us
    dot_general x249 -> x0, matrix products: 183 us -> none  [the longest x235 82.4 us: matmul(): jnp.dot(left_side, right_side, precision=highest, preferred_element_type=...]
    all_gather x2 -> x0, blocking collectives: 166 us -> none  [entering(): gathered = jax.tree.map(lambda a: lax.all_gather(a, axis), part)]
    unnamed x1 -> x0, blocking collectives: 104 us -> none
    another operation x4 -> x0, loops' own time: 72.8 us -> none  [the longest x2 67.3 us: entering(): return lax.fori_loop(0, ahead, one, state)]
    pallas_call x0 -> x1, Pallas kernels: none -> 35.4 us  [on_device(): pl.pallas_call(functools.partial(kernel, n_out, n_in), out_shape=[jax.Sha...]
    dynamic_slice x158 -> x0, local copies, waits for them, and re-layouts: 13.5 us -> none  [the longest x30 8.98 us: one(): lax.dynamic_index_in_dim(a, source, 0, False)]
    rev x1 -> x0, local copies, waits for them, and re-layouts: 11.8 us -> none  [on_device(): smooth_powers = power_stack(smooth_gain, steps_here)[::-1]]
    dynamic_update_slice x128 -> x0, local copies, waits for them, and re-layouts: 7.92 us -> none  [forward_run(): return lax.scan(advance, start_state, drives)]
  transfers between devices with their start and end apart: 1 -> 0, of which waited for: 0 -> 0; matrix products, arithmetic and copies ran while one was open for 16% -> 0% of each run, Pallas kernels for 0% -> 0%
where the time goes in v1:
time: 39.2 us; the launch traced here: 39 us
  Pallas kernels  35.4 us (90%)
  local copies, waits for them, and re-layouts  2.95 us (8%)
  between operations  0.64 us (2%)
    pallas_call x1, Pallas kernels, on_device(): pl.pallas_call(functools.partial(kernel, n_out, n_in), out_shape=[jax.Sha...  35.4 us
    unnamed x2, local copies, waits for them, and re-layouts  2.95 us

profile of v1, /device:TPU:0, one launch (start us, length us, event | category | flops | bytes accessed | tf_op | source)
XLA Modules:
  0.0 39.0 jit_solution(4166900662204161812)
XLA Ops:
  0.6 35.4 %smoother.1 = (f32[64,256]{1,0:T(8,128)}, f32[64,256]{1,0:T(8,128)}) custom-call(f32[512,2048]{1,0:T(8,128)} %readings.1, f32[16,16384]{1,0:T(8,128)} %bitcast.4, s32[128,128]{1,0:T(8,128)} %bitcast.5, f32[128,128]{1,0:T(8,128)} %bitcast.6, f32[1,256]{1,0:T(1,128)} %bitcast.7, f32[256,256]{1,0:T(8,128)} %filt.1, f32[256,256]{1,0:T(8,128)} %model.1, ...), custom_call_target="tpu_custom_call" | custom-call | tf_op jit(solution)/shard_map/smoother/pallas_call | solution.py:340
  36.1 1.5 %copy.13 = f32[64,256]{1,0:T(8,128)} copy(f32[64,256]{1,0:T(8,128)} %get-tuple-element.4) | data formatting | bytes 131072
  37.5 1.5 %copy.14 = f32[64,256]{1,0:T(8,128)} copy(f32[64,256]{1,0:T(8,128)} %get-tuple-element.5) | data formatting | bytes 131072

commit v2 on v1

--- a/solution.py
+++ b/solution.py
@@ -116,13 +116,17 @@
 
     scaled = obs_v[...] * lane_row(prec)
     which = lane_row(block)
-    for b in range(ns // blk):
-        high, low = split(jnp.where(which == b, scaled, 0.0))
-        obs_w[0, b * blk : (b + 1) * blk, :] = high
-        obs_w[1, b * blk : (b + 1) * blk, :] = low
+    for col in range(0, sensors, 256):
+        here = slice(col, col + 256)
+        wide = jnp.concatenate(
+            [jnp.where(which[:, here] == b, scaled[:, here], 0.0) for b in range(ns // blk)], axis=0
+        )
+        high, low = split(wide.T)
+        obs_w[0, here, :] = high
+        obs_w[1, here, :] = low
 
     def nt(a, b):
-        return lax.dot_general(a, b, (((1,), (1,)), ((), ())), preferred_element_type=F32)
+        return dot(a, b)
 
     def rs_copy(k):
         return pltpu.make_async_remote_copy(
@@ -136,18 +140,23 @@
 
     def partial_sum(k):
         in_copy(k).wait()
-        high, low = split(chunk[k])
-        part[k] = nt(high, obs_w[0]) + (nt(low, obs_w[0]) + nt(high, obs_w[1]))
+        in_copy(k + 1).wait()
+        high, low = split(chunk[pl.ds(k, 2)].reshape(2 * steps, sensors))
+        both = nt(high, obs_w[0]) + (nt(low, obs_w[0]) + nt(high, obs_w[1]))
+        part[k] = both[:steps]
+        part[k + 1] = both[steps:]
 
     pl.semaphore_wait(barrier, n - 1)
 
-    def reduce_step(k, c):
-        partial_sum(k)
-        rs_copy(k).start()
-        return c
-
-    lax.fori_loop(0, n_in - 1, reduce_step, 0)
-    partial_sum(n_in - 1)
+    def reduce_step(j, c):
+        partial_sum(2 * j)
+        rs_copy(2 * j).start()
+        rs_copy(2 * j + 1).start()
+        return c
+
+    lax.fori_loop(0, n_in // 2 - 1, reduce_step, 0)
+    partial_sum(n_in - 2)
+    rs_copy(n_in - 2).start()
 
     def put(ref, where, value):
         high, low = split(value)
@@ -345,7 +354,7 @@
         scratch_shapes=[
             pltpu.VMEM((n_in, steps, sensors), F32),
             pltpu.VMEM((blk, sensors), F32),
-            pltpu.VMEM((2, ns, sensors), BF16),
+            pltpu.VMEM((2, sensors, ns), BF16),
             pltpu.VMEM((n_in, steps, ns), F32),
             pltpu.VMEM((n_in - 1, steps, ns), F32),
             pltpu.VMEM((steps, ns), F32),

time: 39.2 us -> 36.5 us (0.931)
  Pallas kernels: 35.4 us -> 32.7 us
    pallas_call x1, Pallas kernels: 35.4 us -> 32.7 us  [on_device(): pl.pallas_call(functools.partial(kernel, n_out, n_in), out_shape=[jax.Sha...]
where the time goes in v2:
time: 36.5 us; the launch traced here: 36.3 us
  Pallas kernels  32.7 us (90%)
  local copies, waits for them, and re-layouts  2.95 us (8%)
  between operations  0.64 us (2%)
    pallas_call x1, Pallas kernels, on_device(): pl.pallas_call(functools.partial(kernel, n_out, n_in), out_shape=[jax.Sha...  32.7 us
    unnamed x2, local copies, waits for them, and re-layouts  2.95 us

profile of v2, /device:TPU:0, one launch (start us, length us, event | category | flops | bytes accessed | tf_op | source)
XLA Modules:
  0.0 36.3 jit_solution(4920920900789904173)
XLA Ops:
  0.6 32.7 %smoother.1 = (f32[64,256]{1,0:T(8,128)}, f32[64,256]{1,0:T(8,128)}) custom-call(f32[512,2048]{1,0:T(8,128)} %readings.1, f32[16,16384]{1,0:T(8,128)} %bitcast.4, s32[128,128]{1,0:T(8,128)} %bitcast.5, f32[128,128]{1,0:T(8,128)} %bitcast.6, f32[1,256]{1,0:T(1,128)} %bitcast.7, f32[256,256]{1,0:T(8,128)} %filt.1, f32[256,256]{1,0:T(8,128)} %model.1, ...), custom_call_target="tpu_custom_call" | custom-call | tf_op jit(solution)/shard_map/smoother/pallas_call | solution.py:349
  33.3 1.5 %copy.13 = f32[64,256]{1,0:T(8,128)} copy(f32[64,256]{1,0:T(8,128)} %get-tuple-element.4) | data formatting | bytes 131072
  34.8 1.5 %copy.14 = f32[64,256]{1,0:T(8,128)} copy(f32[64,256]{1,0:T(8,128)} %get-tuple-element.5) | data formatting | bytes 131072
